TPU v7x, 32 devices: a whole 2x2x4 slice. The times are simulated.
32 devices in a mesh: leaf: 32 (over z, y, x, core).
Axes of the slice: x: 2, y: 2, z: 4, core: 2. Of those that a mesh axis runs over, the one named last changes fastest.
Arguments:
- points: bfloat16 [16, 262144], P(None, 'leaf'), may hold values from -6 to 6
- coords: float32 [3, 262144], P(None, 'leaf'), may hold values from 0 to 1, as said below
- basis: bfloat16 [4096, 2048], P('leaf'), may hold values from -0.75 to 0.75
- far_list: int32 [4096, 16], P('leaf'), may hold values from -1 to 4095, as said below
- far_coupling: bfloat16 [4096, 16, 1024], P('leaf'), may hold values from -0.25 to 0.25
- near_list: int32 [4096, 12], P('leaf'), may hold values from -1 to 4095, as said below
- local_transfer: bfloat16 [8128, 1024], P('leaf'), may hold values from -0.875 to 0.875
- top_transfer: bfloat16 [62, 1024], replicated, may hold values from -0.875 to 0.875
- top_coupling: bfloat16 [60, 2, 1024], replicated, may hold values from -0.75 to 0.75
Outputs:
- product: float32 [16, 262144], P(None, 'leaf')
Inputs may be any that keep to these rules, and one draw needn't show every extreme that they name: `far_list`: -1 marks an empty slot; every other entry is a leaf of the leaf's own device or of a device whose index differs from it in exactly one bit (devices hold 128 leaves each, in order). `near_list`: -1 marks an empty slot; slot 0 holds the leaf itself; every other entry is another leaf at most 8 positions away from it in leaf order. `coords`: the points of leaf i lie in cell i of a k-d split of the unit cube that halves x, y, z in turn, by the bits of i from the most significant.
All inputs are finite; a program needn't handle non-finite values.
Results may differ from a plain program's by a relative error of at most 0.0013.
The roundings to bfloat16 on the way count: a program that leaves them out, or rounds other values in their place, can miss the bound.
Values may be sent and summed in bfloat16 or wider, within the bound.
A program may use at most 128 MiB of HBM per device.

v0:
```python
import functools
import math

import jax
import jax.numpy as jnp
from jax import lax
from jax.experimental import pallas as pl
from jax.experimental.pallas import tpu as pltpu
from jax.sharding import PartitionSpec as P

LEAF = 64
RANK = 32
NF = 16
NN = 12
SPAN = 8
OCT = 8
HALO = SPAN * LEAF
GROUP = 8
EACH = 2
MESH = pl.DeviceIdType.MESH

variance = 1.0
nugget = 0.5
decay_rate = math.sqrt(3.0) / 0.3
f32 = jnp.float32
bf16 = jnp.bfloat16


def top_start(height, number):
    if height == 0:
        return 0
    return 2 * number - number // 2 ** (height - 1)


def halves(x):
    high = x.astype(bf16)
    return jnp.concatenate([high, (x - high.astype(f32)).astype(bf16)], 1)


def dot2(matrix, x, dims=((1,), (0,))):
    both = lax.dot_general(matrix, halves(x), (dims, ((), ())), preferred_element_type=f32)
    return both[:, : x.shape[1]] + both[:, x.shape[1] :]


def unfold(rows, work, out, base):
    tiles = rows.shape[1] // 128
    for t in range(tiles):
        work[pl.ds(t, 8, stride=tiles), :] = rows[:, t * 128 : (t + 1) * 128]
    for n in range(8 * tiles // 8):
        v = work[n * 8 : (n + 1) * 8, :]
        for q in range(4):
            out[pl.ds(base + n * 32 + q, 8, stride=4), :] = turned(v, -q * RANK)


def lane_group(rows, lanes, width):
    return lax.broadcasted_iota(jnp.int32, (rows, lanes), 1) // width


def pick(stacked, count, stride, rows, width):
    groups = lane_group(rows, stacked.shape[1], width)
    kept = jnp.zeros((rows, stacked.shape[1]), f32)
    for n in range(count):
        kept = jnp.where(groups == n * stride, stacked[n * rows : (n + 1) * rows], kept)
    return kept


def turned(x, shift):
    shift %= x.shape[1]
    return x if shift == 0 else pltpu.roll(x, shift, 1)


def up_kernel(
    rhs, octs, points_ref, basis_ref, local_ref, coeff_ref, top_ref, rows_ref, brows_ref,
    wide, spread_out, work, bwide, bout, bwork,
):
    width = OCT * rhs
    number = local_ref.shape[0]
    wide[0:number, :] = local_ref[...].astype(f32)
    bwide[...] = basis_ref[...].astype(f32)

    def open_local(block, carry):
        for u in range(2):
            rows = wide[pl.ds(pl.multiple_of((block * 2 + u) * 8, 8), 8), :]
            unfold(rows, work.at[u], spread_out.at[u], 0)
            at = pl.multiple_of((block * 2 + u) * 8 * RANK, 8 * RANK)
            rows_ref[pl.ds(at, 8 * RANK), :] = spread_out[u][:, :RANK].astype(bf16)
        return carry

    lax.fori_loop(0, wide.shape[0] // 16, open_local, 0)

    row = lax.broadcasted_iota(jnp.int32, (width, OCT * LEAF), 0) // rhs
    own = row == lane_group(width, OCT * LEAF, LEAF)
    state = []
    for g in range(octs):
        cols = slice(g * OCT * LEAF, (g + 1) * OCT * LEAF)
        unfold(bwide[g * OCT : (g + 1) * OCT, :], bwork.at[g % 2], bout.at[g % 2], 0)
        brows = bout[g % 2][:, :RANK].astype(bf16)
        brows_ref[cols, :] = brows
        x = points_ref[:, cols].astype(f32)
        spread = jnp.where(own, jnp.concatenate([x] * OCT, 0), 0.0).astype(bf16)
        c = jnp.dot(spread, brows, preferred_element_type=f32).T.astype(bf16)
        coeff_ref[:, g * width : (g + 1) * width] = c
        state.append(c.astype(f32))

    def apply(rows, x, count):
        mine = lax.broadcasted_iota(jnp.int32, (count * RANK, width), 0) // RANK * (OCT // count)
        tiled = jnp.where(mine == lane_group(count * RANK, width, rhs), jnp.concatenate([x] * count, 0), 0.0)
        return dot2(rows, tiled, ((0,), (0,)))

    offset = 0
    count = OCT
    while count >= 1:
        stride = OCT // count
        after = []
        for g in range(octs):
            rows = rows_ref[(offset + g * count) * RANK : (offset + (g + 1) * count) * RANK]
            kept = apply(rows, state[g], count)
            if count > 1:
                kept = kept + turned(kept, -stride * rhs)
            after.append(kept)
        state = after
        offset += octs * count
        count //= 2
    groups = lane_group(RANK, width, rhs)
    x = jnp.zeros((RANK, width), f32)
    for m in range(OCT):
        x = jnp.where(groups == m, turned(state[2 * m] + state[2 * m + 1], m * rhs), x)
    count = OCT
    while count > 1:
        stride = OCT // count
        rows = rows_ref[offset * RANK : (offset + count) * RANK]
        kept = apply(rows, x, count)
        x = kept + turned(kept, -stride * rhs)
        offset += count
        count //= 2
    small = lane_group(8, width, rhs)
    packed = jnp.zeros((8, width), f32)
    for m in range(RANK // 8):
        packed = jnp.where(small == m, turned(x[m * 8 : (m + 1) * 8], m * rhs), packed)
    top_ref[...] = packed


def spread_kernel(
    count, bits, coeff_ref, top_ref, points_ref, coords_ref,
    parts_ref, tops_ref, epoints_ref, ecoords_ref,
    send_sem, recv_sem, own_sem,
):
    me = lax.axis_index("leaf")
    size = points_ref.shape[1]

    def other(step):
        return lax.rem(me + step, count)

    def flipped(b):
        return me + (1 << b) - 2 * (1 << b) * (lax.div(me, 1 << b) % 2)

    barrier = pltpu.get_barrier_semaphore()

    def greet(step, carry):
        pl.semaphore_signal(barrier, inc=1, device_id=(other(step),), device_id_type=MESH)
        return carry

    lax.fori_loop(1, count, greet, 0)
    pl.semaphore_wait(barrier, count - 1)

    copies = []

    def send(src, dst, device):
        n = len(copies)
        copy = pltpu.make_async_remote_copy(
            src_ref=src, dst_ref=dst, send_sem=send_sem.at[n], recv_sem=recv_sem.at[n],
            device_id=(device,), device_id_type=MESH,
        )
        copy.start()
        copies.append(copy)

    for step in range(1, count):
        send(top_ref, tops_ref.at[step], other(step))
    left, right = other(count - 1), other(1)
    send(points_ref.at[:, pl.ds(size - HALO, HALO)], epoints_ref.at[:, pl.ds(0, HALO)], right)
    send(points_ref.at[:, pl.ds(0, HALO)], epoints_ref.at[:, pl.ds(HALO + size, HALO)], left)
    send(coords_ref.at[:, pl.ds(size - HALO, HALO)], ecoords_ref.at[:, pl.ds(0, HALO)], right)
    send(coords_ref.at[:, pl.ds(0, HALO)], ecoords_ref.at[:, pl.ds(HALO + size, HALO)], left)
    for b in reversed(range(bits)):
        send(coeff_ref, parts_ref.at[b + 1], flipped(b))
    own = [
        pltpu.make_async_copy(coeff_ref, parts_ref.at[0], own_sem.at[0]),
        pltpu.make_async_copy(top_ref, tops_ref.at[0], own_sem.at[1]),
        pltpu.make_async_copy(points_ref, epoints_ref.at[:, pl.ds(HALO, size)], own_sem.at[2]),
        pltpu.make_async_copy(coords_ref, ecoords_ref.at[:, pl.ds(HALO, size)], own_sem.at[3]),
    ]
    for copy in own:
        copy.start()
    for copy in own:
        copy.wait()
    for copy in copies:
        copy.wait()


def near_kernel(
    leaves, rhs, idx_ref, points_ref, coords_ref, out_ref, p_ref, qa_ref, qb_ref, x_ref, acc, todo
):
    empty = leaves + 2 * SPAN
    width = 2 * LEAF
    row = lax.broadcasted_iota(jnp.int32, (8, width), 0)
    low_half = lax.broadcasted_iota(jnp.int32, (48, width), 1) < LEAF
    origin = jnp.broadcast_to(coords_ref[:, HALO : HALO + width][:, :1], (8, width))

    def split(f):
        h = f.astype(bf16).astype(f32)
        m = (f - h).astype(bf16).astype(f32)
        return h, m, f - h - m

    def tables(b, own):
        cols = pl.ds(pl.multiple_of(b * width, width), width)
        v = jnp.where(row < 3, decay_rate * (coords_ref[:, cols] - origin), 0.0)
        norm = jnp.sum(v * v, axis=0, keepdims=True)
        one = jnp.ones_like(v)
        h, m, l = split(jnp.where(row < 3, -2.0 * v, jnp.where(row == 3, norm, jnp.where(row == 4, one, 0.0))))
        q = jnp.concatenate([h, m, h, m, l, h], 0)
        r = pltpu.roll(q, LEAF, 1)
        qa_ref[2 * b] = jnp.where(low_half, q, 0.0).astype(bf16)
        qb_ref[2 * b] = jnp.where(low_half, 0.0, r).astype(bf16)
        qa_ref[2 * b + 1] = jnp.where(low_half, r, 0.0).astype(bf16)
        qb_ref[2 * b + 1] = jnp.where(low_half, 0.0, q).astype(bf16)
        x = points_ref[:, cols].astype(f32).T.astype(bf16)
        x_ref[2 * b] = x[:LEAF]
        x_ref[2 * b + 1] = x[LEAF:]
        if own:
            h, m, l = split(jnp.where(row < 3, v, jnp.where(row == 3, one, jnp.where(row == 4, norm, 0.0))))
            p = jnp.concatenate([h, h, m, m, h, l], 0).T.astype(bf16)
            p_ref[2 * b - SPAN] = p[:LEAF]
            p_ref[2 * b + 1 - SPAN] = p[LEAF:]

    for b in range(SPAN // 2):
        tables(b, False)
        tables(b + (leaves + SPAN) // 2, False)

    def own_tables(g, carry):
        for u in range(GROUP):
            tables(SPAN // 2 + g * GROUP + u, True)
        return carry

    lax.fori_loop(0, leaves // 2 // GROUP, own_tables, 0)
    qa_ref[empty] = jnp.zeros(qa_ref.shape[1:], bf16)
    qb_ref[empty] = jnp.zeros(qb_ref.shape[1:], bf16)
    x_ref[empty] = jnp.zeros(x_ref.shape[1:], bf16)
    p_ref[leaves] = jnp.zeros(p_ref.shape[1:], bf16)

    def chunk(leaf, part):
        base = leaf * NN + part * 4
        j = [idx_ref[base + s] for s in range(4)]
        q = jnp.concatenate([qa_ref[j[0]] + qb_ref[j[1]], qa_ref[j[2]] + qb_ref[j[3]]], axis=1)
        t = jnp.dot(p_ref[leaf], q, preferred_element_type=f32)
        t = jnp.maximum(t, 1e-12)
        r = t * lax.rsqrt(t)
        k = ((1.0 + r) * jnp.exp(-r)).astype(bf16)
        x = jnp.concatenate([x_ref[j[s]] for s in range(4)], axis=0)
        return jnp.dot(k, x, preferred_element_type=f32)

    def first(g, carry):
        got = [chunk(g * GROUP + u, 0) for u in range(GROUP)]
        for u in range(GROUP):
            leaf = g * GROUP + u
            acc[leaf] = got[u] + nugget * x_ref[leaf + SPAN].astype(f32)
        return carry

    lax.fori_loop(0, leaves // GROUP, first, 0)

    def scan(g, n):
        for u in range(GROUP):
            leaf = g * GROUP + u
            for part in (1, 2):
                todo[n] = leaf * 4 + part
                n = n + idx_ref[(leaves + 1) * NN + leaf * 2 + part - 1]
        return n

    n = lax.fori_loop(0, leaves // GROUP, scan, 0)
    for u in range(GROUP):
        todo[n + u] = leaves * 4

    def rest(g, carry):
        entries = [todo[g * GROUP + u] for u in range(GROUP)]
        got = [chunk(lax.div(e, 4), lax.rem(e, 4)) for e in entries]
        for u in range(GROUP):
            acc[lax.div(entries[u], 4)] += got[u]
        return carry

    lax.fori_loop(0, lax.div(n + GROUP - 1, GROUP), rest, 0)

    def turn(g, carry):
        for u in range(GROUP):
            b = g * GROUP + u
            block = acc[pl.ds(2 * b, 2)].reshape(width, rhs)
            out_ref[:, pl.ds(pl.multiple_of(b * width, width), width)] = block.T
        return carry

    lax.fori_loop(0, leaves // 2 // GROUP, turn, 0)


def far_kernel(
    count, bits, rhs, octs, idx_ref, coupling_ref, parts_ref, tops_ref, transfer_ref, cousins_ref,
    down_ref, basis_ref, near_ref, out_ref, table, levels, fields, shift, lined, far_at,
    wide, top_rows, picked, cousin_rows, step_rows, work,
):
    g = pl.program_id(0)
    width = OCT * rhs
    leaves = octs * OCT
    groups = lane_group(RANK, width, rhs)

    @pl.when(g == 0)
    def _():
        device = lax.axis_index("leaf")
        source = lax.broadcasted_iota(jnp.int32, (width, OCT * width), 0)
        target = lax.broadcasted_iota(jnp.int32, (width, OCT * width), 1)
        repeat = (source == target // width * rhs + target % rhs).astype(f32).astype(bf16)

        def fill(part, carry):
            for o in range(octs):
                block = parts_ref[part, :, o * width : (o + 1) * width]
                got = jnp.dot(block, repeat, preferred_element_type=f32).astype(bf16)
                for n in range(OCT):
                    table[(part * octs + o) * OCT + n] = got[:, n * width : (n + 1) * width]
            return carry

        lax.fori_loop(0, bits + 1, fill, 0)
        table[(bits + 1) * leaves] = jnp.zeros((RANK, width), bf16)

        for step in range(count):
            packed = tops_ref[step]
            whole = jnp.concatenate([turned(packed, -m * rhs) for m in range(RANK // 8)], 0)
            levels[lax.rem(device - step + count, count)] = whole
        wide[0 : transfer_ref.shape[0], :] = transfer_ref[...].astype(f32)
        blocks = wide.shape[0] // 8
        for b in range(blocks):
            unfold(wide[b * 8 : (b + 1) * 8, :], work.at[b % OCT], top_rows, b * 8 * RANK)
        for height in range(bits - 1):
            at = top_start(height, count) + lax.div(device, 1 << height)
            picked[2 * height : 2 * height + 2, :] = cousins_ref[at].astype(f32)
            steps = top_rows[pl.ds(pl.multiple_of(at * RANK, RANK), RANK), :][:, :RANK]
            step_rows[height] = steps.astype(bf16)
        for b in range(picked.shape[0] // 8):
            unfold(picked[b * 8 : (b + 1) * 8, :], work.at[b % OCT], cousin_rows, b * 8 * RANK)
        number, base = count, 0
        for height in range(bits - 2):
            start = top_start(height, count)
            for m in range(number // 2):
                both = jnp.concatenate([levels[base + 2 * m], levels[base + 2 * m + 1]], 0)
                at = (start + 2 * m) * RANK
                two = top_rows[at : at + 2 * RANK, :][:, :RANK].astype(bf16)
                levels[base + number + m] = dot2(two, both, ((0,), (0,)))
            base += number
            number //= 2
        field = None
        for height in range(bits - 2, -1, -1):
            base = 2 * count - 2 * (count >> height)
            uncle = lax.rem(lax.div(device, 2 << height) + 1, 2) + 2 * lax.div(device, 4 << height)
            term = 0.0
            for side in range(2):
                at = (2 * height + side) * RANK
                matrix = cousin_rows[at : at + RANK, :][:, :RANK].astype(bf16)
                term = term + dot2(matrix, levels[base + 2 * uncle + side])
            field = term if field is None else term + dot2(step_rows[height], field)
        x = jnp.where(groups == 0, field, 0.0)
        offset = 2 * leaves - 4
        cnt = 2
        while cnt <= OCT:
            stride = OCT // cnt
            x = x + turned(x, stride * rhs)
            rows = down_ref[offset * RANK : (offset + cnt) * RANK]
            x = pick(dot2(rows, x), cnt, stride, RANK, rhs)
            cnt *= 2
            offset -= cnt
        offset += cnt
        state = [jnp.where(groups == 0, turned(x, -(o // 2) * rhs), 0.0) for o in range(octs)]
        cnt = 1
        while cnt < OCT:
            stride = OCT // cnt
            offset -= octs * cnt
            after = []
            for o in range(octs):
                x = state[o]
                if cnt > 1:
                    x = x + turned(x, stride * rhs)
                rows = down_ref[(offset + o * cnt) * RANK : (offset + (o + 1) * cnt) * RANK]
                after.append(pick(dot2(rows, x), cnt, stride, RANK, rhs))
            state = after
            cnt *= 2
        for o in range(octs):
            fields[o] = state[o] + turned(state[o], rhs)

    for u in range(EACH):
        o = g * EACH + u
        weights = []
        masks = [(groups == n).astype(f32).astype(bf16) for n in range(OCT)]
        for s in range(NF):
            w = None
            for n in range(OCT):
                got = table[idx_ref[(o * OCT + n) * NF + s]] * masks[n]
                w = got if w is None else w + got
            weights.append(w)
        weights = jnp.concatenate(weights, 0)
        quarter = lane_group(8, 128, RANK)
        for n in range(OCT):
            c = coupling_ref[u * OCT + n].astype(f32)
            for t in range(8):
                shift[u, n, pl.ds(t, NF, stride=8), :] = c[:, t * 128 : (t + 1) * 128]
            for q in range(NF // 4):
                v = [shift[u, n, (q * 4 + s) * 8 : (q * 4 + s + 1) * 8, :] for s in range(4)]
                moved = []
                for a in range(4):
                    y = turned(v[0], (0 - a) * RANK)
                    for s in range(1, 4):
                        y = jnp.where(quarter == s, turned(v[s], (s - a) * RANK), y)
                    moved.append(y)
                lined[u, n * RANK : (n + 1) * RANK, q * 128 : (q + 1) * 128] = jnp.concatenate(moved, 0).astype(bf16)
        far = pick(jnp.dot(lined[u], weights, preferred_element_type=f32), OCT, 1, RANK, rhs)
        for a in range(4):
            far_at[u, pl.ds(a, 8, stride=4), :] = far[a * 8 : (a + 1) * 8]
        rows = down_ref[pl.ds(pl.multiple_of(o * OCT * RANK, OCT * RANK), OCT * RANK), :]
        field = far_at[u] + pick(dot2(rows, fields[o]), OCT, 1, RANK, rhs)
        field = field.T.astype(bf16)
        cols = slice(u * OCT * LEAF, (u + 1) * OCT * LEAF)
        got = lax.dot_general(field, basis_ref[cols, :], (((1,), (1,)), ((), ())), preferred_element_type=f32)
        out_ref[:, cols] = near_ref[:, cols] + pick(got, OCT, 1, rhs, LEAF)


def per_device(
    points, coords, basis, far_list, far_coupling, near_list, local_transfer, top_transfer, top_coupling
):
    rhs = points.shape[0]
    leaves = basis.shape[0]
    octs = leaves // OCT
    width = OCT * rhs
    size = leaves * LEAF
    device = lax.axis_index("leaf")
    count = lax.axis_size("leaf")
    bits = count.bit_length() - 1
    vmem = pl.BlockSpec(memory_space=pltpu.VMEM)
    smem = pl.BlockSpec(memory_space=pltpu.SMEM)
    limit = pltpu.CompilerParams(vmem_limit_bytes=48 * 2**20)

    def room(n):
        return -(-n // 16) * 16

    nodes = room(local_transfer.shape[0])
    coords8 = jnp.pad(coords, ((0, 5), (0, 0)))

    coeff, top, down, brows = pl.pallas_call(
        functools.partial(up_kernel, rhs, octs),
        out_shape=(
            jax.ShapeDtypeStruct((RANK, leaves * rhs), bf16),
            jax.ShapeDtypeStruct((8, width), f32),
            jax.ShapeDtypeStruct((nodes * RANK, RANK), bf16),
            jax.ShapeDtypeStruct((size, RANK), bf16),
        ),
        in_specs=[vmem] * 3,
        out_specs=(vmem,) * 4,
        scratch_shapes=[
            pltpu.VMEM((nodes, RANK * RANK), f32),
            pltpu.VMEM((2, 8 * RANK, 128), f32),
            pltpu.VMEM((2, 64, 128), f32),
            pltpu.VMEM((leaves, LEAF * RANK), f32),
            pltpu.VMEM((2, OCT * LEAF, 128), f32),
            pltpu.VMEM((2, 128, 128), f32),
        ],
        compiler_params=limit,
        name="up",
    )(points, basis, local_transfer)

    total = count - 1 + 4 + bits
    parts, tops, ext_points, ext_coords = pl.pallas_call(
        functools.partial(spread_kernel, count, bits),
        out_shape=(
            jax.ShapeDtypeStruct((bits + 1, RANK, leaves * rhs), bf16),
            jax.ShapeDtypeStruct((count, 8, width), f32),
            jax.ShapeDtypeStruct((rhs, size + 2 * HALO), bf16),
            jax.ShapeDtypeStruct((8, size + 2 * HALO), f32),
        ),
        in_specs=[vmem] * 4,
        out_specs=(vmem,) * 4,
        scratch_shapes=[
            pltpu.SemaphoreType.DMA((total,)),
            pltpu.SemaphoreType.DMA((total,)),
            pltpu.SemaphoreType.DMA((4,)),
        ],
        compiler_params=pltpu.CompilerParams(
            vmem_limit_bytes=48 * 2**20, collective_id=0, has_side_effects=True
        ),
        name="spread",
    )(coeff, top, points, coords8)

    ext_leaves = leaves + 2 * SPAN
    near_idx = jnp.where(near_list >= 0, near_list - device * leaves + SPAN, ext_leaves)
    used = (jnp.max(near_list[:, 4:].reshape(leaves, 2, 4), axis=2) >= 0).astype(jnp.int32)
    near_idx = jnp.pad(near_idx, ((0, 1), (0, 0)), constant_values=ext_leaves).reshape(-1)
    near_idx = jnp.concatenate([near_idx, used.reshape(-1)])
    near_part = pl.pallas_call(
        functools.partial(near_kernel, leaves, rhs),
        out_shape=jax.ShapeDtypeStruct((rhs, size), f32),
        in_specs=[smem, vmem, vmem],
        out_specs=vmem,
        scratch_shapes=[
            pltpu.VMEM((leaves + 1, LEAF, 48), bf16),
            pltpu.VMEM((ext_leaves + 1, 48, 2 * LEAF), bf16),
            pltpu.VMEM((ext_leaves + 1, 48, 2 * LEAF), bf16),
            pltpu.VMEM((ext_leaves + 1, LEAF, rhs), bf16),
            pltpu.VMEM((leaves + 1, LEAF, rhs), f32),
            pltpu.SMEM((2 * leaves + GROUP + 8,), jnp.int32),
        ],
        compiler_params=limit,
        name="near",
    )(near_idx, ext_points, ext_coords)

    apart = jnp.bitwise_xor(far_list // leaves, device)
    place = sum(jnp.where(apart == 1 << b, b + 1, 0) for b in range(bits))
    far_idx = jnp.where(far_list >= 0, place * leaves + far_list % leaves, (bits + 1) * leaves).reshape(-1)
    whole = lambda *shape: pl.BlockSpec(shape, lambda g: (0,) * len(shape))
    return pl.pallas_call(
        functools.partial(far_kernel, count, bits, rhs, octs),
        grid=(octs // EACH,),
        out_shape=jax.ShapeDtypeStruct((rhs, size), f32),
        in_specs=[
            smem,
            pl.BlockSpec((EACH * OCT, NF, RANK * RANK), lambda g: (g, 0, 0)),
            whole(*parts.shape),
            whole(*tops.shape),
            whole(*top_transfer.shape),
            whole(*top_coupling.shape),
            whole(*down.shape),
            pl.BlockSpec((EACH * OCT * LEAF, RANK), lambda g: (g, 0)),
            pl.BlockSpec((rhs, EACH * OCT * LEAF), lambda g: (0, g)),
        ],
        out_specs=pl.BlockSpec((rhs, EACH * OCT * LEAF), lambda g: (0, g)),
        scratch_shapes=[
            pltpu.VMEM(((bits + 1) * leaves + 1, RANK, width), bf16),
            pltpu.VMEM((2 * count, RANK, width), f32),
            pltpu.VMEM((octs, RANK, width), f32),
            pltpu.VMEM((EACH, OCT, 8 * NF, 128), f32),
            pltpu.VMEM((EACH, OCT * RANK, NF * RANK), bf16),
            pltpu.VMEM((EACH, RANK, width), f32),
            pltpu.VMEM((room(top_transfer.shape[0]), RANK * RANK), f32),
            pltpu.VMEM((room(top_transfer.shape[0]) * RANK, 128), f32),
            pltpu.VMEM((room(2 * bits), RANK * RANK), f32),
            pltpu.VMEM((room(2 * bits) * RANK, 128), f32),
            pltpu.VMEM((bits, RANK, RANK), bf16),
            pltpu.VMEM((OCT, 64, 128), f32),
        ],
        compiler_params=limit,
        name="far",
    )(far_idx, far_coupling, parts, tops, top_transfer, top_coupling, down, brows, near_part)


def solution(mesh):
    return jax.shard_map(
        per_device,
        mesh=mesh,
        in_specs=(
            P(None, "leaf"),
            P(None, "leaf"),
            P("leaf", None),
            P("leaf", None),
            P("leaf", None, None),
            P("leaf", None),
            P("leaf", None),
            P(),
            P(),
        ),
        out_specs=P(None, "leaf"),
        check_vma=False,
    )
```

profile of v0, /device:TPU:0, one launch (start us, length us, event | category | flops | bytes accessed | tf_op | source)
XLA Modules:
  0.0 78.9 jit_solution(13928474588194259574)
XLA Ops:
  0.0 0.0 copy-start.2
  0.0 0.9 %copy-done.2 = bf16[16,8192]{1,0:T(8,128)(2,1)S(1)} copy-done((bf16[16,8192]{1,0:T(8,128)(2,1)S(1)}, bf16[16,8192]{1,0:T(8,128)(2,1)}, u32[]{:S(2)}) %copy-start.2) | copy-done | bytes 262168
  1.0 0.0 copy-start.3
  1.0 1.0 %copy-done.3 = bf16[128,2048]{1,0:T(8,128)(2,1)S(1)} copy-done((bf16[128,2048]{1,0:T(8,128)(2,1)S(1)}, bf16[128,2048]{1,0:T(8,128)(2,1)}, u32[]{:S(2)}) %copy-start.3) | copy-done | bytes 524312
  2.0 0.0 copy-start.4
  2.0 1.0 %copy-done.4 = bf16[254,1024]{1,0:T(8,128)(2,1)S(1)} copy-done((bf16[254,1024]{1,0:T(8,128)(2,1)S(1)}, bf16[254,1024]{1,0:T(8,128)(2,1)}, u32[]{:S(2)}) %copy-start.4) | copy-done | bytes 520216
  3.0 6.6 %up.1 = (bf16[32,2048]{1,0:T(8,128)(2,1)S(1)}, f32[8,128]{1,0:T(8,128)S(1)}, bf16[8192,32]{1,0:T(8,128)(2,1)S(1)}, bf16[8192,32]{1,0:T(8,128)(2,1)S(1)}) custom-call(bf16[16,8192]{1,0:T(8,128)(2,1)S(1)} %copy-done.2, bf16[128,2048]{1,0:T(8,128)(2,1)S(1)} %copy-done.3, bf16[254,1024]{1,0:T(8,128)(2,1)S(1)} %copy-done.4), custom_call_target="tpu_custom_call" | custom-call | tf_op jit(solution)/shard_map/up/pallas_call | solution.py:449
  9.6 1.4 %copy-done = bf16[8192,32]{1,0:T(8,128)(2,1)} copy-done((bf16[8192,32]{1,0:T(8,128)(2,1)}, bf16[8192,32]{1,0:T(8,128)(2,1)S(1)}, u32[]{:S(2)}) %copy-start) | copy-done | bytes 524312
  11.0 0.9 %pad.8.coords_ref = f32[8,8192]{1,0:T(8,128)S(1)} pad(f32[3,8192]{1,0:T(4,128)} %param.10, f32[]{:T(128)} %constant.59.clone.1), padding=0_5x0_0 | pad | bytes 360452 | tf_op jit(solution)/shard_map/jit(_pad)/pad | solution.py:447
  11.9 18.3 %spread.1 = (bf16[6,32,2048]{2,1,0:T(8,128)(2,1)S(1)}, f32[32,8,128]{2,1,0:T(8,128)S(1)}, bf16[16,9216]{1,0:T(8,128)(2,1)S(1)}, f32[8,9216]{1,0:T(8,128)S(1)}) custom-call(bf16[32,2048]{1,0:T(8,128)(2,1)S(1)} %get-tuple-element.13.coeff_ref, f32[8,128]{1,0:T(8,128)S(1)} %get-tuple-element.14.top_ref, bf16[16,8192]{1,0:T(8,128)(2,1)S(1)} %copy-done.2, ...), custom_call_target="tpu_custom_call" | custom-call | tf_op jit(solution)/shard_map/spread/pallas_call | solution.py:472
  30.2 0.0 copy-start.5
  30.2 0.7 copy-done.5
  30.9 0.7 copy-done.7
  31.6 0.6 copy-done.11
  32.3 0.0 copy-done.13
  32.3 0.1 copy.15
  32.4 0.1 reshape.16
  32.5 0.1 copy.14
  32.6 0.1 reshape.18
  32.8 0.1 pad_add_fusion.idx_ref
  32.9 1.0 %copy-done.6 = bf16[16,9216]{1,0:T(8,128)(2,1)S(1)} copy-done((bf16[16,9216]{1,0:T(8,128)(2,1)S(1)}, bf16[16,9216]{1,0:T(8,128)(2,1)}, u32[]{:S(2)}) %copy-start.6) | copy-done | bytes 294936
  33.8 1.0 %copy-done.8 = f32[8,9216]{1,0:T(8,128)S(1)} copy-done((f32[8,9216]{1,0:T(8,128)S(1)}, f32[8,9216]{1,0:T(8,128)}, u32[]{:S(2)}) %copy-start.8) | copy-done | bytes 294936
  34.8 19.6 %near.1.near_ref = f32[16,8192]{1,0:T(8,128)S(1)} custom-call(s32[1804]{0:T(1024)S(1)} %pad_add_fusion.idx_ref, bf16[16,9216]{1,0:T(8,128)(2,1)S(1)} %copy-done.6, f32[8,9216]{1,0:T(8,128)S(1)} %copy-done.8), custom_call_target="tpu_custom_call" | custom-call | tf_op jit(solution)/shard_map/near/pallas_call | solution.py:498
  54.4 0.0 copy-done.14
  54.4 0.7 copy.12
  55.2 0.9 %reshape.15.idx_ref = s32[2048]{0:T(1024)S(1)} reshape(s32[128,16]{1,0:T(8,128)} %copy.12) | data formatting | bytes 16384 | tf_op jit(solution)/shard_map/reshape | solution.py:517
  56.1 0.0 copy-done.10
  56.1 0.0 copy-start.1
  56.1 1.6 %copy-done.1 = bf16[8192,32]{1,0:T(8,128)(2,1)S(1)} copy-done((bf16[8192,32]{1,0:T(8,128)(2,1)S(1)}, bf16[8192,32]{1,0:T(8,128)(2,1)}, u32[]{:S(2)}) %copy-start.1) | copy-done | bytes 524312
  57.7 0.9 %copy-done.9 = bf16[60,2,1024]{2,1,0:T(2,128)(2,1)S(1)} copy-done((bf16[60,2,1024]{2,1,0:T(2,128)(2,1)S(1)}, bf16[60,2,1024]{2,1,0:T(2,128)(2,1)}, u32[]{:S(2)}) %copy-start.9) | copy-done | bytes 245784
  58.6 0.9 %copy-done.12 = f32[32,8,128]{2,1,0:T(8,128)S(1)} copy-done((f32[32,8,128]{2,1,0:T(8,128)S(1)}, f32[32,8,128]{2,1,0:T(8,128)}, u32[]{:S(2)}) %copy-start.12) | copy-done | bytes 131096
  59.5 19.4 %far.1 = f32[16,8192]{1,0:T(8,128)} custom-call(s32[2048]{0:T(1024)S(1)} %reshape.15.idx_ref, bf16[128,16,1024]{2,1,0:T(8,128)(2,1)} %coupling_ref.1, bf16[6,32,2048]{2,1,0:T(8,128)(2,1)S(1)} %get-tuple-element.15.parts_ref, f32[32,8,128]{2,1,0:T(8,128)S(1)} %copy-done.12, bf16[62,1024]{1,0:T(8,128)(2,1)S(1)} %copy-done.10, ...), custom_call_target="tpu_custom_call" | custom-call | tf_op jit(solution)/shard_map/far/pallas_call | solution.py:519
  (16 shorter events, 0.1 us)
Async XLA Ops:
  0.0 0.9 %copy-start.2 = (bf16[16,8192]{1,0:T(8,128)(2,1)S(1)}, bf16[16,8192]{1,0:T(8,128)(2,1)}, u32[]{:S(2)}) copy-start(bf16[16,8192]{1,0:T(8,128)(2,1)} %points_ref.3) | copy-start | bytes 786436
  1.0 1.0 %copy-start.3 = (bf16[128,2048]{1,0:T(8,128)(2,1)S(1)}, bf16[128,2048]{1,0:T(8,128)(2,1)}, u32[]{:S(2)}) copy-start(bf16[128,2048]{1,0:T(8,128)(2,1)} %basis_ref.1) | copy-start | bytes 1572868
  2.0 1.0 %copy-start.4 = (bf16[254,1024]{1,0:T(8,128)(2,1)S(1)}, bf16[254,1024]{1,0:T(8,128)(2,1)}, u32[]{:S(2)}) copy-start(bf16[254,1024]{1,0:T(8,128)(2,1)} %local_ref.1) | copy-start | bytes 1560580
  3.0 29.2 %copy-start.13 = (s32[128,12]{0,1:T(8,128)S(1)}, s32[128,12]{0,1:T(8,128)}, u32[]{:S(2)}) copy-start(s32[128,12]{0,1:T(8,128)} %param.14) | copy-start | bytes 18436
  3.0 51.4 %copy-start.14 = (s32[128,16]{0,1:T(8,128)S(1)}, s32[128,16]{0,1:T(8,128)}, u32[]{:S(2)}) copy-start(s32[128,16]{0,1:T(8,128)} %param.12) | copy-start | bytes 24580
  3.0 53.1 %copy-start.10 = (bf16[62,1024]{1,0:T(8,128)(2,1)S(1)}, bf16[62,1024]{1,0:T(8,128)(2,1)}, u32[]{:S(2)}) copy-start(bf16[62,1024]{1,0:T(8,128)(2,1)} %transfer_ref.1) | copy-start | bytes 380932
  9.6 1.4 %copy-start = (bf16[8192,32]{1,0:T(8,128)(2,1)}, bf16[8192,32]{1,0:T(8,128)(2,1)S(1)}, u32[]{:S(2)}) copy-start(bf16[8192,32]{1,0:T(8,128)(2,1)S(1)} %get-tuple-element.18.basis_ref) | copy-start | bytes 1572868
  30.2 0.7 copy-start.5
  30.9 0.7 copy-start.7
  31.6 0.6 copy-start.11
  32.9 1.0 %copy-start.6 = (bf16[16,9216]{1,0:T(8,128)(2,1)S(1)}, bf16[16,9216]{1,0:T(8,128)(2,1)}, u32[]{:S(2)}) copy-start(bf16[16,9216]{1,0:T(8,128)(2,1)} %copy-done.5) | copy-start | bytes 884740
  33.8 1.0 %copy-start.8 = (f32[8,9216]{1,0:T(8,128)S(1)}, f32[8,9216]{1,0:T(8,128)}, u32[]{:S(2)}) copy-start(f32[8,9216]{1,0:T(8,128)} %copy-done.7) | copy-start | bytes 884740
  56.1 1.6 %copy-start.1 = (bf16[8192,32]{1,0:T(8,128)(2,1)S(1)}, bf16[8192,32]{1,0:T(8,128)(2,1)}, u32[]{:S(2)}) copy-start(bf16[8192,32]{1,0:T(8,128)(2,1)} %copy-done) | copy-start | bytes 1572868
  57.7 0.9 %copy-start.9 = (bf16[60,2,1024]{2,1,0:T(2,128)(2,1)S(1)}, bf16[60,2,1024]{2,1,0:T(2,128)(2,1)}, u32[]{:S(2)}) copy-start(bf16[60,2,1024]{2,1,0:T(2,128)(2,1)} %cousins_ref.1) | copy-start | bytes 737284
  58.6 0.9 %copy-start.12 = (f32[32,8,128]{2,1,0:T(8,128)S(1)}, f32[32,8,128]{2,1,0:T(8,128)}, u32[]{:S(2)}) copy-start(f32[32,8,128]{2,1,0:T(8,128)} %copy-done.11) | copy-start | bytes 393220
where the time goes:
time: 79.8 us; the launch traced here: 78.9 us
  Pallas kernels  63.8 us (80%)
  local copies, waits for them, and re-layouts  14.9 us (19%)
    pallas_call x1, Pallas kernels, per_device(): pl.pallas_call(functools.partial(near_kernel, leaves, rhs), out_shape=jax...  19.6 us
    pallas_call x1, Pallas kernels, per_device(): pl.pallas_call(functools.partial(far_kernel, count, bits, rhs, octs), gri...  19.4 us
    pallas_call x1, Pallas kernels, per_device(): pl.pallas_call(functools.partial(spread_kernel, count, bits), out_shape=(...  18.3 us
    unnamed x31, local copies, waits for them, and re-layouts  11.9 us
    pallas_call x1, Pallas kernels, per_device(): pl.pallas_call(functools.partial(up_kernel, rhs, octs), out_shape=(jax.Sh...  6.58 us

commit v1 on v0

--- a/solution.py
+++ b/solution.py
@@ -140,10 +140,10 @@
     top_ref[...] = packed
 
 
-def spread_kernel(
-    count, bits, coeff_ref, top_ref, points_ref, coords_ref,
-    parts_ref, tops_ref, epoints_ref, ecoords_ref,
-    send_sem, recv_sem, own_sem,
+def near_kernel(
+    count, bits, leaves, rhs, list_ref, coeff_ref, top_ref, points_ref, coords_ref,
+    parts_ref, tops_ref, out_ref,
+    wide, halo_points, halo_coords, p_ref, qa_ref, qb_ref, x_ref, acc, send_sem, recv_sem, own_sem,
 ):
     me = lax.axis_index("leaf")
     size = points_ref.shape[1]
@@ -152,7 +152,7 @@
         return lax.rem(me + step, count)
 
     def flipped(b):
-        return me + (1 << b) - 2 * (1 << b) * (lax.div(me, 1 << b) % 2)
+        return me + (1 << b) - 2 * (1 << b) * lax.rem(lax.div(me, 1 << b), 2)
 
     barrier = pltpu.get_barrier_semaphore()
 
@@ -161,6 +161,8 @@
         return carry
 
     lax.fori_loop(1, count, greet, 0)
+    wide[0:3, :] = coords_ref[...]
+    wide[3:8, :] = jnp.zeros((5, size), f32)
     pl.semaphore_wait(barrier, count - 1)
 
     copies = []
@@ -174,46 +176,35 @@
         copy.start()
         copies.append(copy)
 
+    left, right = other(count - 1), other(1)
+    send(points_ref.at[:, pl.ds(size - HALO, HALO)], halo_points.at[0], right)
+    send(points_ref.at[:, pl.ds(0, HALO)], halo_points.at[1], left)
+    send(wide.at[:, pl.ds(size - HALO, HALO)], halo_coords.at[0], right)
+    send(wide.at[:, pl.ds(0, HALO)], halo_coords.at[1], left)
+    for b in reversed(range(bits)):
+        send(coeff_ref, parts_ref.at[b + 1], flipped(b))
     for step in range(1, count):
         send(top_ref, tops_ref.at[step], other(step))
-    left, right = other(count - 1), other(1)
-    send(points_ref.at[:, pl.ds(size - HALO, HALO)], epoints_ref.at[:, pl.ds(0, HALO)], right)
-    send(points_ref.at[:, pl.ds(0, HALO)], epoints_ref.at[:, pl.ds(HALO + size, HALO)], left)
-    send(coords_ref.at[:, pl.ds(size - HALO, HALO)], ecoords_ref.at[:, pl.ds(0, HALO)], right)
-    send(coords_ref.at[:, pl.ds(0, HALO)], ecoords_ref.at[:, pl.ds(HALO + size, HALO)], left)
-    for b in reversed(range(bits)):
-        send(coeff_ref, parts_ref.at[b + 1], flipped(b))
-    own = [
+    own_copies = [
         pltpu.make_async_copy(coeff_ref, parts_ref.at[0], own_sem.at[0]),
         pltpu.make_async_copy(top_ref, tops_ref.at[0], own_sem.at[1]),
-        pltpu.make_async_copy(points_ref, epoints_ref.at[:, pl.ds(HALO, size)], own_sem.at[2]),
-        pltpu.make_async_copy(coords_ref, ecoords_ref.at[:, pl.ds(HALO, size)], own_sem.at[3]),
     ]
-    for copy in own:
+    for copy in own_copies:
         copy.start()
-    for copy in own:
-        copy.wait()
-    for copy in copies:
-        copy.wait()
-
-
-def near_kernel(
-    leaves, rhs, idx_ref, points_ref, coords_ref, out_ref, p_ref, qa_ref, qb_ref, x_ref, acc, todo
-):
+
     empty = leaves + 2 * SPAN
     width = 2 * LEAF
     row = lax.broadcasted_iota(jnp.int32, (8, width), 0)
     low_half = lax.broadcasted_iota(jnp.int32, (48, width), 1) < LEAF
-    origin = jnp.broadcast_to(coords_ref[:, HALO : HALO + width][:, :1], (8, width))
+    origin = jnp.broadcast_to(wide[:, 0:width][:, :1], (8, width))
 
     def split(f):
         h = f.astype(bf16).astype(f32)
         m = (f - h).astype(bf16).astype(f32)
         return h, m, f - h - m
 
-    def tables(b, own):
-        cols = pl.ds(pl.multiple_of(b * width, width), width)
-        v = jnp.where(row < 3, decay_rate * (coords_ref[:, cols] - origin), 0.0)
+    def tables(b, own, pts, xyz):
+        v = jnp.where(row < 3, decay_rate * (xyz - origin), 0.0)
         norm = jnp.sum(v * v, axis=0, keepdims=True)
         one = jnp.ones_like(v)
         h, m, l = split(jnp.where(row < 3, -2.0 * v, jnp.where(row == 3, norm, jnp.where(row == 4, one, 0.0))))
@@ -223,7 +214,7 @@
         qb_ref[2 * b] = jnp.where(low_half, 0.0, r).astype(bf16)
         qa_ref[2 * b + 1] = jnp.where(low_half, r, 0.0).astype(bf16)
         qb_ref[2 * b + 1] = jnp.where(low_half, 0.0, q).astype(bf16)
-        x = points_ref[:, cols].astype(f32).T.astype(bf16)
+        x = pts.astype(f32).T.astype(bf16)
         x_ref[2 * b] = x[:LEAF]
         x_ref[2 * b + 1] = x[LEAF:]
         if own:
@@ -232,61 +223,53 @@
             p_ref[2 * b - SPAN] = p[:LEAF]
             p_ref[2 * b + 1 - SPAN] = p[LEAF:]
 
-    for b in range(SPAN // 2):
-        tables(b, False)
-        tables(b + (leaves + SPAN) // 2, False)
-
-    def own_tables(g, carry):
-        for u in range(GROUP):
-            tables(SPAN // 2 + g * GROUP + u, True)
-        return carry
-
-    lax.fori_loop(0, leaves // 2 // GROUP, own_tables, 0)
     qa_ref[empty] = jnp.zeros(qa_ref.shape[1:], bf16)
     qb_ref[empty] = jnp.zeros(qb_ref.shape[1:], bf16)
     x_ref[empty] = jnp.zeros(x_ref.shape[1:], bf16)
-    p_ref[leaves] = jnp.zeros(p_ref.shape[1:], bf16)
-
-    def chunk(leaf, part):
-        base = leaf * NN + part * 4
-        j = [idx_ref[base + s] for s in range(4)]
-        q = jnp.concatenate([qa_ref[j[0]] + qb_ref[j[1]], qa_ref[j[2]] + qb_ref[j[3]]], axis=1)
-        t = jnp.dot(p_ref[leaf], q, preferred_element_type=f32)
-        t = jnp.maximum(t, 1e-12)
-        r = t * lax.rsqrt(t)
-        k = ((1.0 + r) * jnp.exp(-r)).astype(bf16)
-        x = jnp.concatenate([x_ref[j[s]] for s in range(4)], axis=0)
-        return jnp.dot(k, x, preferred_element_type=f32)
-
-    def first(g, carry):
-        got = [chunk(g * GROUP + u, 0) for u in range(GROUP)]
+
+    def own_tables(g, carry):
+        for u in range(GROUP):
+            b = g * GROUP + u
+            cols = pl.ds(pl.multiple_of(b * width, width), width)
+            tables(SPAN // 2 + b, True, points_ref[:, cols], wide[:, cols])
+        return carry
+
+    lax.fori_loop(0, leaves // 2 // GROUP, own_tables, 0)
+    base = me * leaves - SPAN
+
+    def leaf_product(leaf):
+        t = []
+        x = []
+        for part in range(NN // 4):
+            j = []
+            for s in range(4):
+                entry = list_ref[leaf, part * 4 + s]
+                j.append(jnp.where(entry >= 0, jnp.clip(entry - base, 0, empty), empty))
+                x.append(x_ref[j[s]])
+            q = jnp.concatenate([qa_ref[j[0]] + qb_ref[j[1]], qa_ref[j[2]] + qb_ref[j[3]]], axis=1)
+            v = jnp.dot(p_ref[leaf], q, preferred_element_type=f32)
+            v = jnp.maximum(v, 1e-12)
+            r = v * lax.rsqrt(v)
+            t.append(((1.0 + r) * jnp.exp(-r)).astype(bf16))
+        return jnp.dot(jnp.concatenate(t, 1), jnp.concatenate(x, 0), preferred_element_type=f32)
+
+    def group(g, carry):
+        got = [leaf_product(g * GROUP + u) for u in range(GROUP)]
         for u in range(GROUP):
             leaf = g * GROUP + u
             acc[leaf] = got[u] + nugget * x_ref[leaf + SPAN].astype(f32)
         return carry
 
-    lax.fori_loop(0, leaves // GROUP, first, 0)
-
-    def scan(g, n):
-        for u in range(GROUP):
-            leaf = g * GROUP + u
-            for part in (1, 2):
-                todo[n] = leaf * 4 + part
-                n = n + idx_ref[(leaves + 1) * NN + leaf * 2 + part - 1]
-        return n
-
-    n = lax.fori_loop(0, leaves // GROUP, scan, 0)
-    for u in range(GROUP):
-        todo[n + u] = leaves * 4
-
-    def rest(g, carry):
-        entries = [todo[g * GROUP + u] for u in range(GROUP)]
-        got = [chunk(lax.div(e, 4), lax.rem(e, 4)) for e in entries]
-        for u in range(GROUP):
-            acc[lax.div(entries[u], 4)] += got[u]
-        return carry
-
-    lax.fori_loop(0, lax.div(n + GROUP - 1, GROUP), rest, 0)
+    lax.fori_loop(SPAN // GROUP, (leaves - SPAN) // GROUP, group, 0)
+    for n in range(4):
+        copies[n].wait()
+    for side in range(2):
+        for b in range(SPAN // 2):
+            cols = slice(b * width, (b + 1) * width)
+            at = b + side * (leaves + SPAN) // 2
+            tables(at, False, halo_points[side, :, cols], halo_coords[side, :, cols])
+    lax.fori_loop(0, SPAN // GROUP, group, 0)
+    lax.fori_loop((leaves - SPAN) // GROUP, leaves // GROUP, group, 0)
 
     def turn(g, carry):
         for u in range(GROUP):
@@ -296,12 +279,16 @@
         return carry
 
     lax.fori_loop(0, leaves // 2 // GROUP, turn, 0)
+    for copy in own_copies:
+        copy.wait()
+    for copy in copies[4:]:
+        copy.wait()
 
 
 def far_kernel(
     count, bits, rhs, octs, idx_ref, coupling_ref, parts_ref, tops_ref, transfer_ref, cousins_ref,
     down_ref, basis_ref, near_ref, out_ref, table, levels, fields, shift, lined, far_at,
-    wide, top_rows, picked, cousin_rows, step_rows, work,
+    wide, top_rows, picked, cousin_rows, step_rows, work, lut,
 ):
     g = pl.program_id(0)
     width = OCT * rhs
@@ -311,6 +298,10 @@
     @pl.when(g == 0)
     def _():
         device = lax.axis_index("leaf")
+        lut[0] = (bits + 1) * leaves - (leaves - 1)
+        lut[device + 1] = 0
+        for b in range(bits):
+            lut[jnp.bitwise_xor(device, 1 << b) + 1] = (b + 1) * leaves
         source = lax.broadcasted_iota(jnp.int32, (width, OCT * width), 0)
         target = lax.broadcasted_iota(jnp.int32, (width, OCT * width), 1)
         repeat = (source == target // width * rhs + target % rhs).astype(f32).astype(bf16)
@@ -396,7 +387,9 @@
         for s in range(NF):
             w = None
             for n in range(OCT):
-                got = table[idx_ref[(o * OCT + n) * NF + s]] * masks[n]
+                entry = idx_ref[o * OCT + n, s]
+                at = lut[lax.div(entry + leaves, leaves)] + jnp.bitwise_and(entry, leaves - 1)
+                got = table[at] * masks[n]
                 w = got if w is None else w + got
             weights.append(w)
         weights = jnp.concatenate(weights, 0)
@@ -433,7 +426,6 @@
     octs = leaves // OCT
     width = OCT * rhs
     size = leaves * LEAF
-    device = lax.axis_index("leaf")
     count = lax.axis_size("leaf")
     bits = count.bit_length() - 1
     vmem = pl.BlockSpec(memory_space=pltpu.VMEM)
@@ -444,8 +436,6 @@
         return -(-n // 16) * 16
 
     nodes = room(local_transfer.shape[0])
-    coords8 = jnp.pad(coords, ((0, 5), (0, 0)))
-
     coeff, top, down, brows = pl.pallas_call(
         functools.partial(up_kernel, rhs, octs),
         out_shape=(
@@ -469,52 +459,35 @@
     )(points, basis, local_transfer)
 
     total = count - 1 + 4 + bits
-    parts, tops, ext_points, ext_coords = pl.pallas_call(
-        functools.partial(spread_kernel, count, bits),
+    ext_leaves = leaves + 2 * SPAN
+    parts, tops, near_part = pl.pallas_call(
+        functools.partial(near_kernel, count, bits, leaves, rhs),
         out_shape=(
             jax.ShapeDtypeStruct((bits + 1, RANK, leaves * rhs), bf16),
             jax.ShapeDtypeStruct((count, 8, width), f32),
-            jax.ShapeDtypeStruct((rhs, size + 2 * HALO), bf16),
-            jax.ShapeDtypeStruct((8, size + 2 * HALO), f32),
+            jax.ShapeDtypeStruct((rhs, size), f32),
         ),
-        in_specs=[vmem] * 4,
-        out_specs=(vmem,) * 4,
+        in_specs=[smem] + [vmem] * 4,
+        out_specs=(vmem,) * 3,
         scratch_shapes=[
+            pltpu.VMEM((8, size), f32),
+            pltpu.VMEM((2, rhs, HALO), bf16),
+            pltpu.VMEM((2, 8, HALO), f32),
+            pltpu.VMEM((leaves, LEAF, 48), bf16),
+            pltpu.VMEM((ext_leaves + 1, 48, 2 * LEAF), bf16),
+            pltpu.VMEM((ext_leaves + 1, 48, 2 * LEAF), bf16),
+            pltpu.VMEM((ext_leaves + 1, LEAF, rhs), bf16),
+            pltpu.VMEM((leaves, LEAF, rhs), f32),
             pltpu.SemaphoreType.DMA((total,)),
             pltpu.SemaphoreType.DMA((total,)),
-            pltpu.SemaphoreType.DMA((4,)),
+            pltpu.SemaphoreType.DMA((2,)),
         ],
         compiler_params=pltpu.CompilerParams(
             vmem_limit_bytes=48 * 2**20, collective_id=0, has_side_effects=True
         ),
-        name="spread",
-    )(coeff, top, points, coords8)
-
-    ext_leaves = leaves + 2 * SPAN
-    near_idx = jnp.where(near_list >= 0, near_list - device * leaves + SPAN, ext_leaves)
-    used = (jnp.max(near_list[:, 4:].reshape(leaves, 2, 4), axis=2) >= 0).astype(jnp.int32)
-    near_idx = jnp.pad(near_idx, ((0, 1), (0, 0)), constant_values=ext_leaves).reshape(-1)
-    near_idx = jnp.concatenate([near_idx, used.reshape(-1)])
-    near_part = pl.pallas_call(
-        functools.partial(near_kernel, leaves, rhs),
-        out_shape=jax.ShapeDtypeStruct((rhs, size), f32),
-        in_specs=[smem, vmem, vmem],
-        out_specs=vmem,
-        scratch_shapes=[
-            pltpu.VMEM((leaves + 1, LEAF, 48), bf16),
-            pltpu.VMEM((ext_leaves + 1, 48, 2 * LEAF), bf16),
-            pltpu.VMEM((ext_leaves + 1, 48, 2 * LEAF), bf16),
-            pltpu.VMEM((ext_leaves + 1, LEAF, rhs), bf16),
-            pltpu.VMEM((leaves + 1, LEAF, rhs), f32),
-            pltpu.SMEM((2 * leaves + GROUP + 8,), jnp.int32),
-        ],
-        compiler_params=limit,
         name="near",
-    )(near_idx, ext_points, ext_coords)
-
-    apart = jnp.bitwise_xor(far_list // leaves, device)
-    place = sum(jnp.where(apart == 1 << b, b + 1, 0) for b in range(bits))
-    far_idx = jnp.where(far_list >= 0, place * leaves + far_list % leaves, (bits + 1) * leaves).reshape(-1)
+    )(near_list, coeff, top, points, coords)
+
     whole = lambda *shape: pl.BlockSpec(shape, lambda g: (0,) * len(shape))
     return pl.pallas_call(
         functools.partial(far_kernel, count, bits, rhs, octs),
@@ -545,10 +518,11 @@
             pltpu.VMEM((room(2 * bits) * RANK, 128), f32),
             pltpu.VMEM((bits, RANK, RANK), bf16),
             pltpu.VMEM((OCT, 64, 128), f32),
+            pltpu.SMEM((count + 1,), jnp.int32),
         ],
         compiler_params=limit,
         name="far",
-    )(far_idx, far_coupling, parts, tops, top_transfer, top_coupling, down, brows, near_part)
+    )(far_list, far_coupling, parts, tops, top_transfer, top_coupling, down, brows, near_part)
 
 
 def solution(mesh):

time: 79.8 us -> 68.9 us (0.86)
  local copies, waits for them, and re-layouts: 14.9 us -> 6.52 us
  Pallas kernels: 63.8 us -> 62 us
    pallas_call x2 -> x1, Pallas kernels: 37.9 us -> 31.1 us  [per_device(): pl.pallas_call(functools.partial(near_kernel, count, bits, leaves, rhs),...]
    unnamed x31 -> x14, local copies, waits for them, and re-layouts: 11.9 us -> 6.52 us
    pallas_call x1, Pallas kernels: 19.4 us -> 24.3 us  [per_device(): pl.pallas_call(functools.partial(far_kernel, count, bits, rhs, octs), gri...]
    reshape x2 -> x0, local copies, waits for them, and re-layouts: 1.02 us -> none  [the longest x1 0.92 us: per_device(): jnp.where(far_list >= 0, place * leaves + far_list % leaves, (bits + 1) *...]
    pad x2 -> x0, local copies, waits for them, and re-layouts: 0.93 us -> none  [the longest x1 0.92 us: per_device(): coords8 = jnp.pad(coords, ((0, 5), (0, 0)))]
where the time goes in v1:
time: 68.9 us; the launch traced here: 68.6 us
  Pallas kernels  62 us (90%)
  local copies, waits for them, and re-layouts  6.52 us (9%)
    pallas_call x1, Pallas kernels, per_device(): pl.pallas_call(functools.partial(near_kernel, count, bits, leaves, rhs),...  31.1 us
    pallas_call x1, Pallas kernels, per_device(): pl.pallas_call(functools.partial(far_kernel, count, bits, rhs, octs), gri...  24.3 us
    pallas_call x1, Pallas kernels, per_device(): pl.pallas_call(functools.partial(up_kernel, rhs, octs), out_shape=(jax.Sh...  6.57 us
    unnamed x14, local copies, waits for them, and re-layouts  6.52 us

profile of v1, /device:TPU:0, one launch (start us, length us, event | category | flops | bytes accessed | tf_op | source)
XLA Modules:
  0.0 68.6 jit_solution(8184223126357991410)
XLA Ops:
  0.0 0.0 copy-start.4
  0.0 0.8 %copy.11.idx_ref = s32[128,16]{1,0:T(8,128)S(1)} copy(s32[128,16]{0,1:T(8,128)} %param.12) | data formatting | bytes 16384 | tf_op args[3]
  0.8 0.8 %copy.10.list_ref = s32[128,12]{1,0:T(8,128)S(1)} copy(s32[128,12]{0,1:T(8,128)} %param.14) | data formatting | bytes 12288 | tf_op args[5]
  1.6 0.0 copy-start
  1.6 0.9 %copy-done = bf16[16,8192]{1,0:T(8,128)(2,1)S(1)} copy-done((bf16[16,8192]{1,0:T(8,128)(2,1)S(1)}, bf16[16,8192]{1,0:T(8,128)(2,1)}, u32[]{:S(2)}) %copy-start) | copy-done | bytes 262168
  2.6 0.0 copy-start.1
  2.6 1.0 %copy-done.1 = bf16[128,2048]{1,0:T(8,128)(2,1)S(1)} copy-done((bf16[128,2048]{1,0:T(8,128)(2,1)S(1)}, bf16[128,2048]{1,0:T(8,128)(2,1)}, u32[]{:S(2)}) %copy-start.1) | copy-done | bytes 524312
  3.6 0.0 copy-start.2
  3.6 1.0 %copy-done.2 = bf16[254,1024]{1,0:T(8,128)(2,1)S(1)} copy-done((bf16[254,1024]{1,0:T(8,128)(2,1)S(1)}, bf16[254,1024]{1,0:T(8,128)(2,1)}, u32[]{:S(2)}) %copy-start.2) | copy-done | bytes 520216
  4.7 6.6 %up.1 = (bf16[32,2048]{1,0:T(8,128)(2,1)S(1)}, f32[8,128]{1,0:T(8,128)S(1)}, bf16[8192,32]{1,0:T(8,128)(2,1)S(1)}, bf16[8192,32]{1,0:T(8,128)(2,1)S(1)}) custom-call(bf16[16,8192]{1,0:T(8,128)(2,1)S(1)} %copy-done, bf16[128,2048]{1,0:T(8,128)(2,1)S(1)} %copy-done.1, bf16[254,1024]{1,0:T(8,128)(2,1)S(1)} %copy-done.2), custom_call_target="tpu_custom_call" | custom-call | tf_op jit(solution)/shard_map/up/pallas_call | solution.py:439
  11.2 0.0 copy-start.5
  11.2 0.9 %copy-done.5 = f32[3,8192]{1,0:T(4,128)S(1)} copy-done((f32[3,8192]{1,0:T(4,128)S(1)}, f32[3,8192]{1,0:T(4,128)}, u32[]{:S(2)}) %copy-start.5) | copy-done | bytes 98328
  12.2 31.1 %near.1 = (bf16[6,32,2048]{2,1,0:T(8,128)(2,1)S(1)}, f32[32,8,128]{2,1,0:T(8,128)S(1)}, f32[16,8192]{1,0:T(8,128)S(1)}) custom-call(s32[128,12]{1,0:T(8,128)S(1)} %copy.10.list_ref, bf16[32,2048]{1,0:T(8,128)(2,1)S(1)} %get-tuple-element.12.coeff_ref, f32[8,128]{1,0:T(8,128)S(1)} %get-tuple-element.13.top_ref, bf16[16,8192]{1,0:T(8,128)(2,1)S(1)} %copy-done, ...), custom_call_target="tpu_custom_call" | custom-call | tf_op jit(solution)/shard_map/near/pallas_call | solution.py:463
  43.3 0.0 copy-done.4
  43.3 0.0 copy-start.3
  43.3 0.9 %copy-done.3 = bf16[60,2,1024]{2,1,0:T(2,128)(2,1)S(1)} copy-done((bf16[60,2,1024]{2,1,0:T(2,128)(2,1)S(1)}, bf16[60,2,1024]{2,1,0:T(2,128)(2,1)}, u32[]{:S(2)}) %copy-start.3) | copy-done | bytes 245784
  44.2 24.3 %far.1 = f32[16,8192]{1,0:T(8,128)} custom-call(s32[128,16]{1,0:T(8,128)S(1)} %copy.11.idx_ref, bf16[128,16,1024]{2,1,0:T(8,128)(2,1)} %coupling_ref.1, bf16[6,32,2048]{2,1,0:T(8,128)(2,1)S(1)} %get-tuple-element.14.parts_ref, f32[32,8,128]{2,1,0:T(8,128)S(1)} %get-tuple-element.15.tops_ref, bf16[62,1024]{1,0:T(8,128)(2,1)S(1)} %copy-done.4, ...), custom_call_target="tpu_custom_call" | custom-call | tf_op jit(solution)/shard_map/far/pallas_call | solution.py:492
Async XLA Ops:
  0.0 43.3 %copy-start.4 = (bf16[62,1024]{1,0:T(8,128)(2,1)S(1)}, bf16[62,1024]{1,0:T(8,128)(2,1)}, u32[]{:S(2)}) copy-start(bf16[62,1024]{1,0:T(8,128)(2,1)} %transfer_ref.1) | copy-start | bytes 380932
  1.6 0.9 %copy-start = (bf16[16,8192]{1,0:T(8,128)(2,1)S(1)}, bf16[16,8192]{1,0:T(8,128)(2,1)}, u32[]{:S(2)}) copy-start(bf16[16,8192]{1,0:T(8,128)(2,1)} %points_ref.3) | copy-start | bytes 786436
  2.6 1.0 %copy-start.1 = (bf16[128,2048]{1,0:T(8,128)(2,1)S(1)}, bf16[128,2048]{1,0:T(8,128)(2,1)}, u32[]{:S(2)}) copy-start(bf16[128,2048]{1,0:T(8,128)(2,1)} %basis_ref.1) | copy-start | bytes 1572868
  3.6 1.0 %copy-start.2 = (bf16[254,1024]{1,0:T(8,128)(2,1)S(1)}, bf16[254,1024]{1,0:T(8,128)(2,1)}, u32[]{:S(2)}) copy-start(bf16[254,1024]{1,0:T(8,128)(2,1)} %local_ref.1) | copy-start | bytes 1560580
  11.2 0.9 %copy-start.5 = (f32[3,8192]{1,0:T(4,128)S(1)}, f32[3,8192]{1,0:T(4,128)}, u32[]{:S(2)}) copy-start(f32[3,8192]{1,0:T(4,128)} %coords_ref.1) | copy-start | bytes 294916
  43.3 0.9 %copy-start.3 = (bf16[60,2,1024]{2,1,0:T(2,128)(2,1)S(1)}, bf16[60,2,1024]{2,1,0:T(2,128)(2,1)}, u32[]{:S(2)}) copy-start(bf16[60,2,1024]{2,1,0:T(2,128)(2,1)} %cousins_ref.1) | copy-start | bytes 737284

commit v2 on v1

--- a/solution.py
+++ b/solution.py
@@ -16,7 +16,7 @@
 OCT = 8
 HALO = SPAN * LEAF
 GROUP = 8
-EACH = 2
+EACH = 4
 MESH = pl.DeviceIdType.MESH
 
 variance = 1.0
@@ -79,14 +79,14 @@
     bwide[...] = basis_ref[...].astype(f32)
 
     def open_local(block, carry):
-        for u in range(2):
-            rows = wide[pl.ds(pl.multiple_of((block * 2 + u) * 8, 8), 8), :]
+        for u in range(4):
+            rows = wide[pl.ds(pl.multiple_of((block * 4 + u) * 8, 8), 8), :]
             unfold(rows, work.at[u], spread_out.at[u], 0)
-            at = pl.multiple_of((block * 2 + u) * 8 * RANK, 8 * RANK)
+            at = pl.multiple_of((block * 4 + u) * 8 * RANK, 8 * RANK)
             rows_ref[pl.ds(at, 8 * RANK), :] = spread_out[u][:, :RANK].astype(bf16)
         return carry
 
-    lax.fori_loop(0, wide.shape[0] // 16, open_local, 0)
+    lax.fori_loop(0, wide.shape[0] // 32, open_local, 0)
 
     row = lax.broadcasted_iota(jnp.int32, (width, OCT * LEAF), 0) // rhs
     own = row == lane_group(width, OCT * LEAF, LEAF)
@@ -235,7 +235,6 @@
         return carry
 
     lax.fori_loop(0, leaves // 2 // GROUP, own_tables, 0)
-    base = me * leaves - SPAN
 
     def leaf_product(leaf):
         t = []
@@ -243,8 +242,7 @@
         for part in range(NN // 4):
             j = []
             for s in range(4):
-                entry = list_ref[leaf, part * 4 + s]
-                j.append(jnp.where(entry >= 0, jnp.clip(entry - base, 0, empty), empty))
+                j.append(list_ref[leaf, part * 4 + s])
                 x.append(x_ref[j[s]])
             q = jnp.concatenate([qa_ref[j[0]] + qb_ref[j[1]], qa_ref[j[2]] + qb_ref[j[3]]], axis=1)
             v = jnp.dot(p_ref[leaf], q, preferred_element_type=f32)
@@ -288,7 +286,7 @@
 def far_kernel(
     count, bits, rhs, octs, idx_ref, coupling_ref, parts_ref, tops_ref, transfer_ref, cousins_ref,
     down_ref, basis_ref, near_ref, out_ref, table, levels, fields, shift, lined, far_at,
-    wide, top_rows, picked, cousin_rows, step_rows, work, lut,
+    wide, top_rows, picked, cousin_rows, step_rows, work,
 ):
     g = pl.program_id(0)
     width = OCT * rhs
@@ -298,10 +296,6 @@
     @pl.when(g == 0)
     def _():
         device = lax.axis_index("leaf")
-        lut[0] = (bits + 1) * leaves - (leaves - 1)
-        lut[device + 1] = 0
-        for b in range(bits):
-            lut[jnp.bitwise_xor(device, 1 << b) + 1] = (b + 1) * leaves
         source = lax.broadcasted_iota(jnp.int32, (width, OCT * width), 0)
         target = lax.broadcasted_iota(jnp.int32, (width, OCT * width), 1)
         repeat = (source == target // width * rhs + target % rhs).astype(f32).astype(bf16)
@@ -387,9 +381,7 @@
         for s in range(NF):
             w = None
             for n in range(OCT):
-                entry = idx_ref[o * OCT + n, s]
-                at = lut[lax.div(entry + leaves, leaves)] + jnp.bitwise_and(entry, leaves - 1)
-                got = table[at] * masks[n]
+                got = table[idx_ref[o * OCT + n, s]] * masks[n]
                 w = got if w is None else w + got
             weights.append(w)
         weights = jnp.concatenate(weights, 0)
@@ -426,6 +418,7 @@
     octs = leaves // OCT
     width = OCT * rhs
     size = leaves * LEAF
+    device = lax.axis_index("leaf")
     count = lax.axis_size("leaf")
     bits = count.bit_length() - 1
     vmem = pl.BlockSpec(memory_space=pltpu.VMEM)
@@ -433,7 +426,7 @@
     limit = pltpu.CompilerParams(vmem_limit_bytes=48 * 2**20)
 
     def room(n):
-        return -(-n // 16) * 16
+        return -(-n // 32) * 32
 
     nodes = room(local_transfer.shape[0])
     coeff, top, down, brows = pl.pallas_call(
@@ -448,8 +441,8 @@
         out_specs=(vmem,) * 4,
         scratch_shapes=[
             pltpu.VMEM((nodes, RANK * RANK), f32),
-            pltpu.VMEM((2, 8 * RANK, 128), f32),
-            pltpu.VMEM((2, 64, 128), f32),
+            pltpu.VMEM((4, 8 * RANK, 128), f32),
+            pltpu.VMEM((4, 64, 128), f32),
             pltpu.VMEM((leaves, LEAF * RANK), f32),
             pltpu.VMEM((2, OCT * LEAF, 128), f32),
             pltpu.VMEM((2, 128, 128), f32),
@@ -460,6 +453,11 @@
 
     total = count - 1 + 4 + bits
     ext_leaves = leaves + 2 * SPAN
+    near_idx = jnp.where(near_list >= 0, near_list - device * leaves + SPAN, ext_leaves)
+    apart = jnp.bitwise_xor(jnp.right_shift(far_list, leaves.bit_length() - 1), device)
+    place = sum(jnp.where(apart == 1 << b, (b + 1) * leaves, 0) for b in range(bits))
+    far_idx = place + jnp.bitwise_and(far_list, leaves - 1)
+    far_idx = jnp.where(far_list >= 0, far_idx, (bits + 1) * leaves)
     parts, tops, near_part = pl.pallas_call(
         functools.partial(near_kernel, count, bits, leaves, rhs),
         out_shape=(
@@ -486,7 +484,7 @@
             vmem_limit_bytes=48 * 2**20, collective_id=0, has_side_effects=True
         ),
         name="near",
-    )(near_list, coeff, top, points, coords)
+    )(near_idx, coeff, top, points, coords)
 
     whole = lambda *shape: pl.BlockSpec(shape, lambda g: (0,) * len(shape))
     return pl.pallas_call(
@@ -518,11 +516,10 @@
             pltpu.VMEM((room(2 * bits) * RANK, 128), f32),
             pltpu.VMEM((bits, RANK, RANK), bf16),
             pltpu.VMEM((OCT, 64, 128), f32),
-            pltpu.SMEM((count + 1,), jnp.int32),
         ],
         compiler_params=limit,
         name="far",
-    )(far_list, far_coupling, parts, tops, top_transfer, top_coupling, down, brows, near_part)
+    )(far_idx, far_coupling, parts, tops, top_transfer, top_coupling, down, brows, near_part)
 
 
 def solution(mesh):

time: 68.9 us -> 63.1 us (0.916)
  Pallas kernels: 62 us -> 54.4 us
  other arithmetic: 0 us -> 2.91 us
  local copies, waits for them, and re-layouts: 6.52 us -> 5.22 us
    pallas_call x1, Pallas kernels: 24.3 us -> 18.3 us  [per_device(): pl.pallas_call(functools.partial(far_kernel, count, bits, rhs, octs), gri...]
    unnamed x14 -> x13, local copies, waits for them, and re-layouts: 6.52 us -> 4.75 us
    ge x0 -> x2, other arithmetic: none -> 1.45 us  [the longest x1 0.75 us: per_device(): near_list >= 0]
    pallas_call x1, Pallas kernels: 31.1 us -> 30.2 us  [per_device(): pl.pallas_call(functools.partial(near_kernel, count, bits, leaves, rhs),...]
    add x0 -> x1, other arithmetic: none -> 0.7 us  [per_device(): near_list - device * leaves + SPAN]
    shift_right_arithmetic x0 -> x1, other arithmetic: none -> 0.7 us  [per_device(): jnp.right_shift(far_list, leaves.bit_length() - 1)]
where the time goes in v2:
time: 63.1 us; the launch traced here: 62.6 us
  Pallas kernels  54.4 us (86%)
  local copies, waits for them, and re-layouts  5.22 us (8%)
  other arithmetic  2.91 us (5%)
    pallas_call x1, Pallas kernels, per_device(): pl.pallas_call(functools.partial(near_kernel, count, bits, leaves, rhs),...  30.2 us
    pallas_call x1, Pallas kernels, per_device(): pl.pallas_call(functools.partial(far_kernel, count, bits, rhs, octs), gri...  18.3 us
    pallas_call x1, Pallas kernels, per_device(): pl.pallas_call(functools.partial(up_kernel, rhs, octs), out_shape=(jax.Sh...  5.93 us
    unnamed x13, local copies, waits for them, and re-layouts  4.75 us

profile of v2, /device:TPU:0, one launch (start us, length us, event | category | flops | bytes accessed | tf_op | source)
XLA Modules:
  0.0 62.6 jit_solution(5578720622407465159)
XLA Ops:
  0.0 0.0 copy-start.3
  0.0 0.0 copy-start.4
  0.0 0.8 %broadcast_compare_fusion.1 = pred[128,12]{0,1:T(8,128)(4,1)S(1)} fusion(s32[128,12]{0,1:T(8,128)} %param.14), kind=kLoop, calls=%fused_computation.4 | loop fusion | flops 1536 | bytes 7680 | tf_op jit(solution)/shard_map/ge | solution.py:456
  0.8 0.7 %broadcast_compare_fusion = pred[128,16]{0,1:T(8,128)(4,1)S(1)} fusion(s32[128,16]{0,1:T(8,128)} %param.12), kind=kLoop, calls=%fused_computation.3 | loop fusion | flops 2048 | bytes 10240 | tf_op jit(solution)/shard_map/ge | solution.py:460
  1.5 0.7 %subtract_add_fusion = s32[128,12]{0,1:T(8,128)S(1)} fusion(s32[128,12]{0,1:T(8,128)} %param.14, s32[]{:T(128)S(6)} %mul.3), kind=kLoop, calls=%fused_computation.2 | loop fusion | flops 3072 | bytes 12292 | tf_op jit(solution)/shard_map/add | solution.py:456
  2.2 0.7 %broadcast_shift-right-arithmetic_fusion = s32[128,16]{0,1:T(8,128)S(1)} fusion(s32[128,16]{0,1:T(8,128)} %param.12), kind=kLoop, calls=%fused_computation.5 | loop fusion | flops 2048 | bytes 16384 | tf_op jit(solution)/shard_map/shift_right_arithmetic | solution.py:457
  2.9 0.1 copy.23
  3.0 0.1 copy.24
  3.1 0.1 copy.21
  3.2 0.1 copy.25
  3.3 0.8 %copy.22 = s32[128,16]{1,0:T(8,128)S(1)} copy(s32[128,16]{0,1:T(8,128)} %param.12) | data formatting | bytes 16384 | tf_op args[3]
  4.2 0.0 copy-start
  4.2 0.9 %copy-done = bf16[16,8192]{1,0:T(8,128)(2,1)S(1)} copy-done((bf16[16,8192]{1,0:T(8,128)(2,1)S(1)}, bf16[16,8192]{1,0:T(8,128)(2,1)}, u32[]{:S(2)}) %copy-start) | copy-done | bytes 262168
  5.1 0.0 copy-start.1
  5.2 1.0 %copy-done.1 = bf16[128,2048]{1,0:T(8,128)(2,1)S(1)} copy-done((bf16[128,2048]{1,0:T(8,128)(2,1)S(1)}, bf16[128,2048]{1,0:T(8,128)(2,1)}, u32[]{:S(2)}) %copy-start.1) | copy-done | bytes 524312
  6.2 0.0 copy-start.2
  6.2 1.0 %copy-done.2 = bf16[254,1024]{1,0:T(8,128)(2,1)S(1)} copy-done((bf16[254,1024]{1,0:T(8,128)(2,1)S(1)}, bf16[254,1024]{1,0:T(8,128)(2,1)}, u32[]{:S(2)}) %copy-start.2) | copy-done | bytes 520216
  7.2 5.9 %up.1 = (bf16[32,2048]{1,0:T(8,128)(2,1)S(1)}, f32[8,128]{1,0:T(8,128)S(1)}, bf16[8192,32]{1,0:T(8,128)(2,1)S(1)}, bf16[8192,32]{1,0:T(8,128)(2,1)S(1)}) custom-call(bf16[16,8192]{1,0:T(8,128)(2,1)S(1)} %copy-done, bf16[128,2048]{1,0:T(8,128)(2,1)S(1)} %copy-done.1, bf16[254,1024]{1,0:T(8,128)(2,1)S(1)} %copy-done.2), custom_call_target="tpu_custom_call" | custom-call | tf_op jit(solution)/shard_map/up/pallas_call | solution.py:432
  13.2 0.0 copy-start.5
  13.2 0.9 %copy-done.5 = f32[3,8192]{1,0:T(4,128)S(1)} copy-done((f32[3,8192]{1,0:T(4,128)S(1)}, f32[3,8192]{1,0:T(4,128)}, u32[]{:S(2)}) %copy-start.5) | copy-done | bytes 98328
  14.1 30.2 %near.1 = (bf16[6,32,2048]{2,1,0:T(8,128)(2,1)S(1)}, f32[32,8,128]{2,1,0:T(8,128)S(1)}, f32[16,8192]{1,0:T(8,128)S(1)}) custom-call(s32[128,12]{1,0:T(8,128)S(1)} %broadcast_select_fusion.list_ref, bf16[32,2048]{1,0:T(8,128)(2,1)S(1)} %get-tuple-element.12.coeff_ref, f32[8,128]{1,0:T(8,128)S(1)} %get-tuple-element.13.top_ref, bf16[16,8192]{1,0:T(8,128)(2,1)S(1)} %copy-done, ...), custom_call_target="tpu_custom_call" | custom-call | tf_op jit(solution)/shard_map/near/pallas_call | solution.py:461
  44.3 0.0 copy-done.3
  44.3 0.0 copy-done.4
  44.3 18.3 %far.1 = f32[16,8192]{1,0:T(8,128)} custom-call(s32[128,16]{1,0:T(8,128)S(1)} %add_select_fusion.idx_ref, bf16[128,16,1024]{2,1,0:T(8,128)(2,1)} %coupling_ref.1, bf16[6,32,2048]{2,1,0:T(8,128)(2,1)S(1)} %get-tuple-element.14.parts_ref, f32[32,8,128]{2,1,0:T(8,128)S(1)} %get-tuple-element.15.tops_ref, bf16[62,1024]{1,0:T(8,128)(2,1)S(1)} %copy-done.4, ...), custom_call_target="tpu_custom_call" | custom-call | tf_op jit(solution)/shard_map/far/pallas_call | solution.py:490
  (2 shorter events, 0.1 us)
Async XLA Ops:
  0.0 44.3 %copy-start.3 = (bf16[60,2,1024]{2,1,0:T(2,128)(2,1)S(1)}, bf16[60,2,1024]{2,1,0:T(2,128)(2,1)}, u32[]{:S(2)}) copy-start(bf16[60,2,1024]{2,1,0:T(2,128)(2,1)} %cousins_ref.1) | copy-start | bytes 737284
  0.0 44.3 %copy-start.4 = (bf16[62,1024]{1,0:T(8,128)(2,1)S(1)}, bf16[62,1024]{1,0:T(8,128)(2,1)}, u32[]{:S(2)}) copy-start(bf16[62,1024]{1,0:T(8,128)(2,1)} %transfer_ref.1) | copy-start | bytes 380932
  4.2 1.0 %copy-start = (bf16[16,8192]{1,0:T(8,128)(2,1)S(1)}, bf16[16,8192]{1,0:T(8,128)(2,1)}, u32[]{:S(2)}) copy-start(bf16[16,8192]{1,0:T(8,128)(2,1)} %points_ref.3) | copy-start | bytes 786436
  5.1 1.0 %copy-start.1 = (bf16[128,2048]{1,0:T(8,128)(2,1)S(1)}, bf16[128,2048]{1,0:T(8,128)(2,1)}, u32[]{:S(2)}) copy-start(bf16[128,2048]{1,0:T(8,128)(2,1)} %basis_ref.1) | copy-start | bytes 1572868
  6.2 1.0 %copy-start.2 = (bf16[254,1024]{1,0:T(8,128)(2,1)S(1)}, bf16[254,1024]{1,0:T(8,128)(2,1)}, u32[]{:S(2)}) copy-start(bf16[254,1024]{1,0:T(8,128)(2,1)} %local_ref.1) | copy-start | bytes 1560580
  13.2 0.9 %copy-start.5 = (f32[3,8192]{1,0:T(4,128)S(1)}, f32[3,8192]{1,0:T(4,128)}, u32[]{:S(2)}) copy-start(f32[3,8192]{1,0:T(4,128)} %coords_ref.1) | copy-start | bytes 294916
